TPU v7x, 128 devices: a whole 4x4x4 slice. The times are simulated.
128 devices in a mesh: dev: 128 (over z, x, y, core).
Axes of the slice: x: 4, y: 4, z: 4, core: 2. Of those that a mesh axis runs over, the one named last changes fastest.
Arguments:
- lambda0: float32 [10, 7, 7, 65536], P(None, None, None, 'dev'), may hold values from -6 to 6
- order: int32 [65536], P('dev'), may hold values from 3 to 6
- send_index: int32 [128, 512], P('dev'), may hold values from 0 to 511, each once within a row
- recv_slot: int32 [128, 512], P('dev'), may hold values from 0 to 511, each once within a row
- objective_grad: float32 [10, 7, 7, 65536], P(None, None, None, 'dev'), may hold values from -6 to 6
- metric: float32 [2, 65536], P(None, 'dev'), may hold values from 0.03 to 0.1
- pseudo_step: float32 [65536], P('dev'), may hold values from 0.05 to 0.25
- couplings: float32 [4, 10, 10], replicated, may hold values from -1.25 to 1.25
- neighbour: int32 [4, 65536], P(None, 'dev'), may hold values from 0 to 1023, as said below
- neighbour_face: int32 [4, 65536], P(None, 'dev'), may hold values from 0 to 3
- orient: int32 [4, 65536], P(None, 'dev'), may hold values from 0 to 1
- halo_send: int32 [2, 32768], P(None, 'dev'), may hold values from 0 to 511, as said below
Outputs:
- adjoint_two: float32 [10, 7, 7, 65536], P(None, None, None, 'dev')
- residual_one: float32 [10, 7, 7, 65536], P(None, None, None, 'dev')
Inputs may be any that keep to these rules, and one draw needn't show every extreme that they name: `send_index`: each row is a permutation of 0 to 511. `recv_slot`: each row is a permutation of 0 to 511. `neighbour`: values 512 + x name position x of the below owner's last-row list, 768 + x position x of the above owner's first-row list; each ghost is named once. `halo_send`: each owner's two lists hold 256 distinct local slots each, slots of that owner.
All inputs are finite; a program needn't handle non-finite values.
Results may differ from a plain program's by a relative error of at most 0.00007.
Values sent between devices are 32-bit elements; how exact they have to be, the bound alone decides.
A program may use at most 128 MiB of HBM per device.

v0:
```python
import functools

import jax
import jax.numpy as jnp
from jax import lax
from jax.experimental import pallas as pl
from jax.experimental.pallas import tpu as pltpu
from jax.sharding import PartitionSpec as P

F = 10
M = 7
E = 512
HALO = 256
PLACE = (0, 2, 4, 6, 1, 3, 5)
EVEN = (0, 2, 4, 6)
ODD = (1, 3, 5)
BLOCK = 8 * F
ROWS = M * BLOCK
NN = (((1,), (0,)), ((), ()))
NT = (((1,), (1,)), ((), ()))
F32 = jnp.float32
BF16 = jnp.bfloat16


def iota(shape, dim):
    return lax.broadcasted_iota(jnp.int32, shape, dim)


def dot(a, b, dims=NN):
    return lax.dot_general(a, b, dims, preferred_element_type=F32)


def exact_dot(a, b, dims=NN):
    return lax.dot_general(
        a, b, dims, precision=lax.Precision.HIGHEST, preferred_element_type=F32
    )


def halves(value):
    high = value.astype(BF16)
    low = (value - high.astype(F32)).astype(BF16)
    return high, low


def one_hot(equal):
    return jnp.where(equal, 1.0, 0.0).astype(BF16)


def column(row):
    return jnp.transpose(jnp.broadcast_to(row.astype(F32), (8, row.shape[1])))[:, 0:1].astype(jnp.int32)


def build_operators(coup, even_ops, odd_ops):
    wide = 384
    r = iota((BLOCK, wide), 0)
    c = iota((BLOCK, wide), 1)
    at = (
        (c >= BLOCK).astype(jnp.int32)
        + (c >= 2 * BLOCK).astype(jnp.int32)
        + (c >= 3 * BLOCK).astype(jnp.int32)
        + (c >= 4 * BLOCK).astype(jnp.int32)
    )
    jr = r & 7
    jc = c & 7
    same_j = jr == jc
    even_sum = ((jr + jc) & 1) == 0
    two_jc = (2 * jc + 1).astype(F32)
    d_j = jnp.where((jc < jr) & ~even_sum, two_jc, 0.0)
    delta_j = jnp.where(same_j, 1.0, 0.0)
    pair_j = jnp.where(even_sum, 2.0, 0.0)
    parity_jc = jnp.where((jc & 1) == 0, 1.0, -1.0)

    spread_f = jnp.where((iota((BLOCK, F), 0) >> 3) == iota((BLOCK, F), 1), 1.0, 0.0)
    cg = iota((F, wide), 1)
    cg_at = (
        (cg >= BLOCK).astype(jnp.int32)
        + (cg >= 2 * BLOCK).astype(jnp.int32)
        + (cg >= 3 * BLOCK).astype(jnp.int32)
        + (cg >= 4 * BLOCK).astype(jnp.int32)
    )
    spread_g = jnp.where(((cg - cg_at * BLOCK) >> 3) == iota((F, wide), 0), 1.0, 0.0)
    c0, c1, c2, c3 = (
        exact_dot(exact_dot(spread_f, coup[k], NT), spread_g) for k in range(4)
    )

    def build(ops, own, other, store):
        first = own[0]
        valid = at < len(own)
        ic = 2 * at + first
        two_ic = (2 * ic + 1).astype(F32)
        zero = jnp.zeros((BLOCK, wide), F32)
        blocks = [
            jnp.where(valid, c3 * delta_j, zero),
            jnp.where(valid & (ic == jr), c3 * parity_jc, zero),
            jnp.where(valid & (ic == jr), c3, zero),
        ]
        for i in other:
            if i > 0:
                blocks.append(jnp.where(valid & (ic < i), c0 * delta_j * two_ic, zero))
        for i in own:
            blocks.append(jnp.where(valid & (ic == i), c1 * d_j, zero))
        for i in own:
            same_i = ic == i
            here = c3 * (2.0 * delta_j + jnp.where(same_i, pair_j, 0.0))
            here = here + jnp.where(same_i, c2 * delta_j, 0.0)
            blocks.append(jnp.where(valid, here, zero))
        for at_row, block in enumerate(blocks):
            store(ops, at_row * BLOCK, block)

    def store_even(ops, row, block):
        high = block.astype(BF16).astype(F32)
        low = block - high
        rows = pl.ds(row, BLOCK)
        ops[rows, 0:256] = high[:, 0:256].astype(BF16)
        shared = high[:, 256:384] + pltpu.roll(low[:, 256:384], 64, 1)
        ops[rows, 256:384] = shared.astype(BF16)
        ops[rows, 384:640] = low[:, 0:256].astype(BF16)
        ops[rows, 640:896] = high[:, 0:256].astype(BF16)
        ops[rows, 896:1024] = high[:, 256:384].astype(BF16)

    def store_odd(ops, row, block):
        high, low = halves(block[:, 0:256])
        rows = pl.ds(row, BLOCK)
        ops[rows, 0:256] = high
        ops[rows, 256:512] = low
        ops[rows, 512:768] = high

    build(even_ops, EVEN, ODD, store_even)
    build(odd_ops, ODD, EVEN, store_odd)


def kernel(
    n,
    lam,
    order,
    send_index,
    recv_slot,
    grad,
    metric,
    step,
    coup,
    neighbour,
    neighbour_face,
    orient,
    halo_send,
    out_two,
    out_res,
    x_in,
    g_in,
    compact,
    send_buf,
    recv_buf,
    oh_slot,
    oh_local,
    oh_ghost,
    oh_halo,
    even_ops,
    odd_ops,
    even_v,
    odd_v,
    field,
    masks,
    traces,
    trace_halves,
    faces_send,
    faces_recv,
    halo_out,
    halo_in,
    even_res,
    odd_res,
    across,
    res_out,
    two_out,
    local_sem,
    move_send,
    move_recv,
    face_send_sem,
    face_recv_sem,
    halo_send_sem,
    halo_recv_sem,
):
    me = lax.axis_index("dev")
    cap = E // n
    chunk = 4 * cap
    above = lax.rem(me + 1, n)
    below = lax.rem(me + n - 1, n)
    barrier = pltpu.get_barrier_semaphore()

    x_copy = pltpu.make_async_copy(lam, x_in, local_sem.at[0])
    x_copy.start()
    g_copy = pltpu.make_async_copy(grad, g_in, local_sem.at[1])
    g_copy.start()

    def greet(j, carry):
        pl.semaphore_signal(barrier, inc=1, device_id=(lax.rem(me + j, n),), device_id_type=pl.DeviceIdType.MESH)
        return carry

    lax.fori_loop(1, n, greet, 0)

    oh_send = one_hot(column(send_index[...]) == iota((E, E), 1))
    tail = jnp.where(iota((E - F * M * M, E), 0) == 0, order[...].astype(F32), 0.0)
    compact[pl.ds(F * M * M, E - F * M * M), :] = tail
    x_copy.wait()
    for at, i in enumerate(PLACE):
        for f in range(F):
            compact[pl.ds(M * (at * F + f), M), :] = x_in[f, i]
    high, low = halves(compact[...])
    sorted_rows = dot(oh_send, high, NT) + dot(oh_send, low, NT)
    for part in range(4):
        send_buf[pl.ds(part, E, stride=4), :] = sorted_rows[:, 128 * part : 128 * (part + 1)]

    pl.semaphore_wait(barrier, n - 1)

    def piece(p):
        return pl.ds(pl.multiple_of(p * chunk, chunk), chunk)

    def move(j, carry):
        p = lax.rem(me + j, n)
        pltpu.make_async_remote_copy(
            src_ref=send_buf.at[piece(p), :],
            dst_ref=recv_buf.at[piece(me), :],
            send_sem=move_send,
            recv_sem=move_recv,
            device_id=(p,),
            device_id_type=pl.DeviceIdType.MESH,
        ).start()
        return carry

    lax.fori_loop(1, n, move, 0)
    own = pltpu.make_async_copy(send_buf.at[piece(me), :], recv_buf.at[piece(me), :], local_sem.at[2])
    own.start()

    rows = iota((E, E), 0)
    for k in range(4):
        name = neighbour[pl.ds(k, 1), :]
        oh_local[:, E * k : E * (k + 1)] = one_hot(rows == name)
        oh_ghost[:, E * k : E * (k + 1)] = one_hot(rows == name - E)
    for side in range(2):
        oh_halo[:, HALO * side : HALO * (side + 1)] = one_hot(
            iota((E, HALO), 0) == halo_send[pl.ds(side, 1), :]
        )

    wanted = jnp.zeros((16, E), F32)
    for k in range(4):
        face_row = jnp.broadcast_to(neighbour_face[pl.ds(k, 1), :].astype(F32), (16, E)).astype(BF16)
        wanted = wanted + dot(face_row, oh_ghost[:, E * k : E * (k + 1)], NT)
    faces_send[0] = wanted[0:8, 0:HALO]
    faces_send[1] = wanted[0:8, HALO:E]
    tell_below = pltpu.make_async_remote_copy(
        src_ref=faces_send.at[0],
        dst_ref=faces_recv.at[1],
        send_sem=face_send_sem.at[0],
        recv_sem=face_recv_sem.at[1],
        device_id=(below,),
        device_id_type=pl.DeviceIdType.MESH,
    )
    tell_above = pltpu.make_async_remote_copy(
        src_ref=faces_send.at[1],
        dst_ref=faces_recv.at[0],
        send_sem=face_send_sem.at[1],
        recv_sem=face_recv_sem.at[0],
        device_id=(above,),
        device_id_type=pl.DeviceIdType.MESH,
    )
    tell_below.start()
    tell_above.start()

    oh_slot[...] = one_hot(column(recv_slot[...]) == iota((E, E), 1))
    build_operators(coup, even_ops, odd_ops)
    even_v[pl.ds(960, 64), :] = jnp.zeros((64, E), BF16)
    for part in range(3):
        odd_v[pl.ds(256 * part + 240, 16), :] = jnp.zeros((16, E), BF16)
    g_copy.wait()
    tell_below.wait()
    tell_above.wait()

    own.wait()
    everyone = pl.ds(0, (n - 1) * chunk)
    arrived = pltpu.make_async_remote_copy(
        src_ref=send_buf.at[everyone, :],
        dst_ref=recv_buf.at[everyone, :],
        send_sem=move_send,
        recv_sem=move_recv,
        device_id=(above,),
        device_id_type=pl.DeviceIdType.MESH,
    )
    arrived.wait_recv()
    for part in range(4):
        flat = jnp.transpose(recv_buf[pl.ds(part, E, stride=4), :])
        high, low = halves(flat)
        compact[pl.ds(128 * part, 128), :] = dot(high, oh_slot[...]) + dot(low, oh_slot[...])

    order_row = compact[pl.ds(F * M * M, 1), :]
    lane_mode = iota((8, E), 0).astype(F32)
    mask_j = jnp.where(lane_mode <= order_row, 1.0, 0.0)
    for i in range(M):
        masks[i] = jnp.where(order_row >= float(i), mask_j, 0.0)

    def keep_halves(at, value):
        high, low = halves(value)
        if at < 3:
            even_v[pl.ds(BLOCK * at, BLOCK), :] = high
        else:
            even_v[pl.ds(240, 16), :] = high[0:16]
            even_v[pl.ds(256, 64), :] = high[16:80]
            even_v[pl.ds(320, 64), :] = high[16:80]
        if at < 3:
            even_v[pl.ds(384 + BLOCK * at, BLOCK), :] = high
        else:
            even_v[pl.ds(384 + 240, 16), :] = high[0:16]
        even_v[pl.ds(640 + BLOCK * at, BLOCK), :] = low

    def keep_odd_halves(at, value):
        high, low = halves(value)
        odd_v[pl.ds(BLOCK * at, BLOCK), :] = high
        odd_v[pl.ds(256 + BLOCK * at, BLOCK), :] = high
        odd_v[pl.ds(512 + BLOCK * at, BLOCK), :] = low

    def set_field(at, value):
        field[pl.ds(BLOCK * at, BLOCK), :] = value
        if at < 4:
            keep_halves(at, value)
        else:
            keep_odd_halves(at - 4, value)

    for at, i in enumerate(PLACE):
        mask = masks[i]
        parts = [compact[pl.ds(M * (at * F + f), 8), :] * mask for f in range(F)]
        set_field(at, jnp.concatenate(parts, axis=0))

    odd_row = (iota((8, E), 0) & 1) == 1
    m0 = metric[pl.ds(0, 1), :]
    m1 = metric[pl.ds(1, 1), :]
    pace = step[...]

    def send_halo(sweep):
        picked = dot(trace_halves[...], oh_halo[...])
        picked = picked[0:320] + picked[320:640]
        for side in range(2):
            face = faces_recv[side][0:1, :]
            lanes = slice(HALO * side, HALO * (side + 1))
            chosen = picked[240:320, lanes]
            for k in (2, 1, 0):
                chosen = jnp.where(face == float(k), picked[80 * k : 80 * (k + 1), lanes], chosen)
            halo_out[sweep, side] = chosen
        down = pltpu.make_async_remote_copy(
            src_ref=halo_out.at[sweep, 0],
            dst_ref=halo_in.at[sweep, 1],
            send_sem=halo_send_sem.at[sweep, 0],
            recv_sem=halo_recv_sem.at[sweep, 1],
            device_id=(below,),
            device_id_type=pl.DeviceIdType.MESH,
        )
        up = pltpu.make_async_remote_copy(
            src_ref=halo_out.at[sweep, 1],
            dst_ref=halo_in.at[sweep, 0],
            send_sem=halo_send_sem.at[sweep, 1],
            recv_sem=halo_recv_sem.at[sweep, 0],
            device_id=(above,),
            device_id_type=pl.DeviceIdType.MESH,
        )
        down.start()
        up.start()
        return down, up

    def residual(sweep, finish):
        from_even = dot(even_ops[pl.ds(0, 240), :], even_v[...])
        from_odd = dot(odd_ops[pl.ds(0, 240), :], odd_v[...])
        traces[0] = from_even[80:160] + from_odd[80:160]
        traces[1] = from_even[0:80] + from_odd[0:80]
        traces[2] = from_even[160:240] + from_odd[160:240]
        traces[3] = from_even[0:80] - from_odd[0:80]
        for k in range(4):
            high, low = halves(traces[k])
            trace_halves[pl.ds(80 * k, 80), :] = high
            trace_halves[pl.ds(320 + 80 * k, 80), :] = low
        down, up = send_halo(sweep)

        for k in range(4):
            got = dot(trace_halves[...], oh_local[:, E * k : E * (k + 1)])
            got = got[0:320] + got[320:640]
            face = neighbour_face[pl.ds(k, 1), :]
            chosen = got[240:320]
            for other in (2, 1, 0):
                chosen = jnp.where(face == other, got[80 * other : 80 * (other + 1)], chosen)
            across[k] = chosen
        even_res[...] = dot(even_ops[pl.ds(240, 880), :], even_v[...])
        odd_res[...] = dot(odd_ops[pl.ds(240, 720), :], odd_v[...])

        down.wait()
        up.wait()
        ghost = jnp.concatenate([halo_in[sweep, 0], halo_in[sweep, 1]], axis=1)
        ghost_halves = jnp.concatenate(list(halves(ghost)), axis=0)
        for k in range(4):
            got = dot(ghost_halves, oh_ghost[:, E * k : E * (k + 1)])
            turned = jnp.where(odd_row & (orient[pl.ds(k, 1), :] == 1), -1.0, 1.0)
            turned = jnp.concatenate([turned] * F, axis=0)
            across[k] = (across[k] + got[0:80] + got[80:160]) * turned
        south = across[0]
        north = across[2]
        across[0] = north + south
        across[2] = north - south
        east = across[1]
        west = across[3]
        across[1] = east + west
        across[3] = east - west

        for at, i in enumerate(PLACE):
            if i % 2 == 0:
                here = m1 * even_res[pl.ds(240 + BLOCK * at, BLOCK), :]
                here = here + even_res[pl.ds(560 + BLOCK * at, BLOCK), :]
                if i > 0:
                    here = here + m0 * odd_res[pl.ds(BLOCK * (at - 1), BLOCK), :]
                here = here - across[1]
            else:
                here = m1 * odd_res[pl.ds(240 + BLOCK * (at - 4), BLOCK), :]
                here = here + odd_res[pl.ds(480 + BLOCK * (at - 4), BLOCK), :]
                here = here + m0 * even_res[pl.ds(BLOCK * (at - 4), BLOCK), :]
                here = here - across[3]
            mask = masks[i]
            parts = []
            for f in range(F):
                plus = jnp.broadcast_to(across[0, pl.ds(8 * f + i, 1), :], (8, E))
                minus = jnp.broadcast_to(across[2, pl.ds(8 * f + i, 1), :], (8, E))
                lift = jnp.where(odd_row, minus, plus)
                goal = jnp.concatenate([g_in[f, i], jnp.zeros((1, E), F32)], axis=0)
                parts.append((here[8 * f : 8 * f + 8] - lift - goal) * mask)
            value = jnp.concatenate(parts, axis=0)
            finish(at, i, value, field[pl.ds(BLOCK * at, BLOCK), :] - pace * value)

    def next_field(at, i, value, advanced):
        set_field(at, advanced)

    def results(at, i, value, advanced):
        for f in range(F):
            res_out[f, i] = value[8 * f : 8 * f + M]
            two_out[f, i] = advanced[8 * f : 8 * f + M]

    residual(0, next_field)
    residual(1, results)
    copy_res = pltpu.make_async_copy(res_out, out_res, local_sem.at[3])
    copy_two = pltpu.make_async_copy(two_out, out_two, local_sem.at[4])
    copy_res.start()
    copy_two.start()
    arrived.wait_send()
    copy_res.wait()
    copy_two.wait()


def shards(n, *args):
    (lam, order, send_index, recv_slot, grad, metric, step, coup, neighbour, neighbour_face, orient, halo_send) = args
    in_vmem = pl.BlockSpec(memory_space=pltpu.VMEM)
    anywhere = pl.BlockSpec(memory_space=pl.ANY)
    shape = jax.ShapeDtypeStruct((F, M, M, E), F32)
    return pl.pallas_call(
        functools.partial(kernel, n),
        out_shape=(shape, shape),
        in_specs=[
            anywhere,
            in_vmem,
            in_vmem,
            in_vmem,
            anywhere,
            in_vmem,
            in_vmem,
            in_vmem,
            in_vmem,
            in_vmem,
            in_vmem,
            in_vmem,
        ],
        out_specs=(anywhere, anywhere),
        scratch_shapes=[
            pltpu.VMEM((F, M, M, E), F32),
            pltpu.VMEM((F, M, M, E), F32),
            pltpu.VMEM((E, E), F32),
            pltpu.VMEM((4 * E, 128), F32),
            pltpu.VMEM((4 * E, 128), F32),
            pltpu.VMEM((E, E), BF16),
            pltpu.VMEM((E, 4 * E), BF16),
            pltpu.VMEM((E, 4 * E), BF16),
            pltpu.VMEM((E, E), BF16),
            pltpu.VMEM((14 * BLOCK, 1024), BF16),
            pltpu.VMEM((12 * BLOCK, 768), BF16),
            pltpu.VMEM((1024, E), BF16),
            pltpu.VMEM((768, E), BF16),
            pltpu.VMEM((ROWS, E), F32),
            pltpu.VMEM((M, 8, E), F32),
            pltpu.VMEM((4, BLOCK, E), F32),
            pltpu.VMEM((8 * BLOCK, E), BF16),
            pltpu.VMEM((2, 8, HALO), F32),
            pltpu.VMEM((2, 8, HALO), F32),
            pltpu.VMEM((2, 2, BLOCK, HALO), F32),
            pltpu.VMEM((2, 2, BLOCK, HALO), F32),
            pltpu.VMEM((11 * BLOCK, E), F32),
            pltpu.VMEM((9 * BLOCK, E), F32),
            pltpu.VMEM((4, BLOCK, E), F32),
            pltpu.VMEM((F, M, M, E), F32),
            pltpu.VMEM((F, M, M, E), F32),
            pltpu.SemaphoreType.DMA((5,)),
            pltpu.SemaphoreType.DMA,
            pltpu.SemaphoreType.DMA,
            pltpu.SemaphoreType.DMA((2,)),
            pltpu.SemaphoreType.DMA((2,)),
            pltpu.SemaphoreType.DMA((2, 2)),
            pltpu.SemaphoreType.DMA((2, 2)),
        ],
        compiler_params=pltpu.CompilerParams(
            collective_id=0, has_side_effects=True, vmem_limit_bytes=48 * 1024 * 1024
        ),
    )(
        lam,
        order.reshape(1, E),
        send_index,
        recv_slot,
        grad,
        metric,
        step.reshape(1, E),
        coup,
        neighbour,
        neighbour_face,
        orient,
        halo_send,
    )


def solution(mesh):
    in_specs = (
        P(None, None, None, "dev"),
        P("dev"),
        P("dev", None),
        P("dev", None),
        P(None, None, None, "dev"),
        P(None, "dev"),
        P("dev"),
        P(),
        P(None, "dev"),
        P(None, "dev"),
        P(None, "dev"),
        P(None, "dev"),
    )
    out_specs = (P(None, None, None, "dev"), P(None, None, None, "dev"))
    return jax.shard_map(
        functools.partial(shards, mesh.shape["dev"]),
        mesh=mesh,
        in_specs=in_specs,
        out_specs=out_specs,
        check_vma=False,
    )
```

profile of v0, /device:TPU:0, one launch (start us, length us, event | category | flops | bytes accessed | tf_op | source)
XLA Modules:
  0.0 56.3 jit_solution(1788853885814898978)
XLA Ops:
  0.6 0.7 %copy.14.coup = f32[4,10,10]{2,1,0:T(8,128)S(1)} copy(f32[4,10,10]{2,0,1:T(4,128)} %param.19) | data formatting | bytes 3200 | tf_op args[7]
  1.4 0.0 copy-start
  1.4 1.3 %copy-done = f32[10,7,7,512]{3,2,1,0:T(8,128)S(1)} copy-done((f32[10,7,7,512]{3,2,1,0:T(8,128)S(1)}, f32[10,7,7,512]{3,2,1,0:T(8,128)}, u32[]{:S(2)}) %copy-start) | copy-done | bytes 1003544
  2.6 0.0 copy-start.1
  2.6 1.3 %copy-done.1 = f32[10,7,7,512]{3,2,1,0:T(8,128)S(1)} copy-done((f32[10,7,7,512]{3,2,1,0:T(8,128)S(1)}, f32[10,7,7,512]{3,2,1,0:T(8,128)}, u32[]{:S(2)}) %copy-start.1) | copy-done | bytes 1003544
  3.9 0.0 copy-start.2
  3.9 0.7 %copy-done.2 = s32[4,512]{1,0:T(4,128)S(1)} copy-done((s32[4,512]{1,0:T(4,128)S(1)}, s32[4,512]{1,0:T(4,128)}, u32[]{:S(2)}) %copy-start.2) | copy-done | bytes 8216
  4.6 0.0 copy-start.3
  4.6 0.7 %copy-done.3 = s32[4,512]{1,0:T(4,128)S(1)} copy-done((s32[4,512]{1,0:T(4,128)S(1)}, s32[4,512]{1,0:T(4,128)}, u32[]{:S(2)}) %copy-start.3) | copy-done | bytes 8216
  5.3 0.0 copy-start.4
  5.3 0.7 %copy-done.4 = s32[4,512]{1,0:T(4,128)S(1)} copy-done((s32[4,512]{1,0:T(4,128)S(1)}, s32[4,512]{1,0:T(4,128)}, u32[]{:S(2)}) %copy-start.4) | copy-done | bytes 8216
  6.0 0.0 copy-start.5
  6.0 0.7 %copy-done.5 = f32[2,512]{1,0:T(2,128)S(1)} copy-done((f32[2,512]{1,0:T(2,128)S(1)}, f32[2,512]{1,0:T(2,128)}, u32[]{:S(2)}) %copy-start.5) | copy-done | bytes 4120
  6.7 0.0 copy-start.6
  6.7 0.7 %copy-done.6 = s32[512]{0:T(512)S(1)} copy-done((s32[512]{0:T(512)S(1)}, s32[512]{0:T(512)}, u32[]{:S(2)}) %copy-start.6) | copy-done | bytes 2072
  7.3 0.0 copy-start.7
  7.3 0.7 %copy-done.7 = s32[1,512]{1,0:T(1,128)S(1)} copy-done((s32[1,512]{1,0:T(1,128)S(1)}, s32[1,512]{1,0:T(1,128)}, u32[]{:S(2)}) %copy-start.7) | copy-done | bytes 2072
  8.0 0.0 copy-start.8
  8.0 0.7 %copy-done.8 = s32[1,512]{1,0:T(1,128)S(1)} copy-done((s32[1,512]{1,0:T(1,128)S(1)}, s32[1,512]{1,0:T(1,128)}, u32[]{:S(2)}) %copy-start.8) | copy-done | bytes 2072
  8.7 0.0 copy-start.9
  8.7 0.7 %copy-done.9 = f32[512]{0:T(512)S(1)} copy-done((f32[512]{0:T(512)S(1)}, f32[512]{0:T(512)}, u32[]{:S(2)}) %copy-start.9) | copy-done | bytes 2072
  9.4 0.0 copy-start.10
  9.4 0.7 %copy-done.10 = s32[2,256]{1,0:T(2,128)S(1)} copy-done((s32[2,256]{1,0:T(2,128)S(1)}, s32[2,256]{1,0:T(2,128)}, u32[]{:S(2)}) %copy-start.10) | copy-done | bytes 2072
  10.1 44.2 %shard_map.131 = (f32[10,7,7,512]{3,2,1,0:T(8,128)S(1)}, f32[10,7,7,512]{3,2,1,0:T(8,128)S(1)}) custom-call(f32[10,7,7,512]{3,2,1,0:T(8,128)S(1)} %copy-done, s32[1,512]{1,0:T(1,128)S(1)} %bitcast.2, s32[1,512]{1,0:T(1,128)S(1)} %copy-done.7, s32[1,512]{1,0:T(1,128)S(1)} %copy-done.8, f32[10,7,7,512]{3,2,1,0:T(8,128)S(1)} %copy-done.1, ...), custom_call_target="tpu_custom_call" | custom-call | tf_op jit(solution)/shard_map/pallas_call | solution.py:455
  54.3 1.0 %copy.17 = f32[10,7,7,512]{3,2,1,0:T(8,128)} copy(f32[10,7,7,512]{3,2,1,0:T(8,128)S(1)} %get-tuple-element.4) | data formatting | bytes 2007040
  55.3 1.0 %copy.18 = f32[10,7,7,512]{3,2,1,0:T(8,128)} copy(f32[10,7,7,512]{3,2,1,0:T(8,128)S(1)} %get-tuple-element.5) | data formatting | bytes 2007040
Async XLA Ops:
  1.4 1.3 %copy-start = (f32[10,7,7,512]{3,2,1,0:T(8,128)S(1)}, f32[10,7,7,512]{3,2,1,0:T(8,128)}, u32[]{:S(2)}) copy-start(f32[10,7,7,512]{3,2,1,0:T(8,128)} %lam.1) | copy-start | bytes 3010564
  2.6 1.3 %copy-start.1 = (f32[10,7,7,512]{3,2,1,0:T(8,128)S(1)}, f32[10,7,7,512]{3,2,1,0:T(8,128)}, u32[]{:S(2)}) copy-start(f32[10,7,7,512]{3,2,1,0:T(8,128)} %grad.1) | copy-start | bytes 3010564
  3.9 0.7 %copy-start.2 = (s32[4,512]{1,0:T(4,128)S(1)}, s32[4,512]{1,0:T(4,128)}, u32[]{:S(2)}) copy-start(s32[4,512]{1,0:T(4,128)} %neighbour.1) | copy-start | bytes 24580
  4.6 0.7 %copy-start.3 = (s32[4,512]{1,0:T(4,128)S(1)}, s32[4,512]{1,0:T(4,128)}, u32[]{:S(2)}) copy-start(s32[4,512]{1,0:T(4,128)} %neighbour_face.1) | copy-start | bytes 24580
  5.3 0.7 %copy-start.4 = (s32[4,512]{1,0:T(4,128)S(1)}, s32[4,512]{1,0:T(4,128)}, u32[]{:S(2)}) copy-start(s32[4,512]{1,0:T(4,128)} %orient.1) | copy-start | bytes 24580
  6.0 0.7 %copy-start.5 = (f32[2,512]{1,0:T(2,128)S(1)}, f32[2,512]{1,0:T(2,128)}, u32[]{:S(2)}) copy-start(f32[2,512]{1,0:T(2,128)} %metric.1) | copy-start | bytes 12292
  6.7 0.7 %copy-start.6 = (s32[512]{0:T(512)S(1)}, s32[512]{0:T(512)}, u32[]{:S(2)}) copy-start(s32[512]{0:T(512)} %param.13) | copy-start | bytes 6148
  7.3 0.7 %copy-start.7 = (s32[1,512]{1,0:T(1,128)S(1)}, s32[1,512]{1,0:T(1,128)}, u32[]{:S(2)}) copy-start(s32[1,512]{1,0:T(1,128)} %send_index.1) | copy-start | bytes 6148
  8.0 0.7 %copy-start.8 = (s32[1,512]{1,0:T(1,128)S(1)}, s32[1,512]{1,0:T(1,128)}, u32[]{:S(2)}) copy-start(s32[1,512]{1,0:T(1,128)} %recv_slot.1) | copy-start | bytes 6148
  8.7 0.7 %copy-start.9 = (f32[512]{0:T(512)S(1)}, f32[512]{0:T(512)}, u32[]{:S(2)}) copy-start(f32[512]{0:T(512)} %param.18) | copy-start | bytes 6148
  9.4 0.7 %copy-start.10 = (s32[2,256]{1,0:T(2,128)S(1)}, s32[2,256]{1,0:T(2,128)}, u32[]{:S(2)}) copy-start(s32[2,256]{1,0:T(2,128)} %halo_send.1) | copy-start | bytes 6148
where the time goes:
time: 56.8 us; the launch traced here: 56.3 us
  Pallas kernels  44.2 us (78%)
  local copies, waits for them, and re-layouts  11.4 us (20%)
  between operations  0.65 us (1%)
    pallas_call x1, Pallas kernels, shards(): pl.pallas_call(functools.partial(kernel, n), out_shape=(shape, shape), in...  44.2 us
    unnamed x25, local copies, waits for them, and re-layouts  11.4 us

commit v1 on v0

--- a/solution.py
+++ b/solution.py
@@ -22,6 +22,40 @@
 BF16 = jnp.bfloat16
 
 
+def send_order(sizes):
+    left = [
+        (a, b, c, d)
+        for d in range(sizes[3])
+        for c in range(sizes[2])
+        for b in range(sizes[1])
+        for a in range(sizes[0])
+    ][1:]
+
+    def hops(offset):
+        load = []
+        for step, size in zip(offset[:3], sizes):
+            back = size - step if step else 0
+            load += [step * (step <= back), back * (back <= step)]
+            if step and step == back:
+                load[-2:] = [step / 2, back / 2]
+        return load
+
+    total = [0.0] * 6
+    order = []
+    while left:
+
+        def score(offset):
+            load = [a + b for a, b in zip(total, hops(offset))]
+            even = max(load) - min(load) + 0.01 * sum(v * v for v in load) / (1 + sum(load))
+            return even - 0.3 * sum(hops(offset))
+
+        best = min(left, key=score)
+        left.remove(best)
+        order.append(best)
+        total = [a + b for a, b in zip(total, hops(best))]
+    return order
+
+
 def iota(shape, dim):
     return lax.broadcasted_iota(jnp.int32, shape, dim)
 
@@ -80,7 +114,7 @@
     )
     spread_g = jnp.where(((cg - cg_at * BLOCK) >> 3) == iota((F, wide), 0), 1.0, 0.0)
     c0, c1, c2, c3 = (
-        exact_dot(exact_dot(spread_f, coup[k], NT), spread_g) for k in range(4)
+        exact_dot(exact_dot(spread_f, coup[:, k, :], NT), spread_g) for k in range(4)
     )
 
     def build(ops, own, other, store):
@@ -132,10 +166,24 @@
 def kernel(
     n,
     lam,
+    order_far,
+    send_far,
+    recv_far,
+    grad,
+    metric_far,
+    step_far,
+    coup_far,
+    neighbour_far,
+    face_far,
+    orient_far,
+    halo_far,
+    two_out,
+    res_out,
+    x_in,
+    g_in,
     order,
     send_index,
     recv_slot,
-    grad,
     metric,
     step,
     coup,
@@ -143,10 +191,6 @@
     neighbour_face,
     orient,
     halo_send,
-    out_two,
-    out_res,
-    x_in,
-    g_in,
     compact,
     send_buf,
     recv_buf,
@@ -169,8 +213,7 @@
     even_res,
     odd_res,
     across,
-    res_out,
-    two_out,
+    input_sem,
     local_sem,
     move_send,
     move_recv,
@@ -186,10 +229,27 @@
     below = lax.rem(me + n - 1, n)
     barrier = pltpu.get_barrier_semaphore()
 
-    x_copy = pltpu.make_async_copy(lam, x_in, local_sem.at[0])
-    x_copy.start()
-    g_copy = pltpu.make_async_copy(grad, g_in, local_sem.at[1])
-    g_copy.start()
+    fetches = [
+        pltpu.make_async_copy(far, near, input_sem.at[at])
+        for at, (far, near) in enumerate(
+            (
+                (send_far, send_index),
+                (order_far, order),
+                (lam, x_in),
+                (neighbour_far, neighbour),
+                (face_far, neighbour_face),
+                (halo_far, halo_send),
+                (recv_far, recv_slot),
+                (coup_far, coup),
+                (orient_far, orient),
+                (metric_far, metric),
+                (step_far, step),
+                (grad, g_in),
+            )
+        )
+    ]
+    for fetch in fetches:
+        fetch.start()
 
     def greet(j, carry):
         pl.semaphore_signal(barrier, inc=1, device_id=(lax.rem(me + j, n),), device_id_type=pl.DeviceIdType.MESH)
@@ -197,10 +257,12 @@
 
     lax.fori_loop(1, n, greet, 0)
 
+    fetches[0].wait()
+    fetches[1].wait()
     oh_send = one_hot(column(send_index[...]) == iota((E, E), 1))
     tail = jnp.where(iota((E - F * M * M, E), 0) == 0, order[...].astype(F32), 0.0)
     compact[pl.ds(F * M * M, E - F * M * M), :] = tail
-    x_copy.wait()
+    fetches[2].wait()
     for at, i in enumerate(PLACE):
         for f in range(F):
             compact[pl.ds(M * (at * F + f), M), :] = x_in[f, i]
@@ -214,8 +276,19 @@
     def piece(p):
         return pl.ds(pl.multiple_of(p * chunk, chunk), chunk)
 
-    def move(j, carry):
-        p = lax.rem(me + j, n)
+    sizes = (n // 32, 4, 4, 2) if n >= 32 else (1, 1, n // 2, 2)
+    core = lax.rem(me, 2)
+    for offset in send_order(sizes):
+        p = lax.rem(core + offset[3], 2)
+        weight = 2
+        place = me // 2
+        for shift, size in zip(offset[2::-1], sizes[2::-1]):
+            here = lax.rem(place, size)
+            if shift:
+                here = lax.rem(here + jnp.where(core == 0, shift, size - shift), size)
+            p = p + weight * here
+            weight = weight * size
+            place = place // size
         pltpu.make_async_remote_copy(
             src_ref=send_buf.at[piece(p), :],
             dst_ref=recv_buf.at[piece(me), :],
@@ -224,12 +297,11 @@
             device_id=(p,),
             device_id_type=pl.DeviceIdType.MESH,
         ).start()
-        return carry
-
-    lax.fori_loop(1, n, move, 0)
-    own = pltpu.make_async_copy(send_buf.at[piece(me), :], recv_buf.at[piece(me), :], local_sem.at[2])
+    own = pltpu.make_async_copy(send_buf.at[piece(me), :], recv_buf.at[piece(me), :], local_sem.at[0])
     own.start()
 
+    for fetch in fetches[3:]:
+        fetch.wait()
     rows = iota((E, E), 0)
     for k in range(4):
         name = neighbour[pl.ds(k, 1), :]
@@ -270,7 +342,6 @@
     even_v[pl.ds(960, 64), :] = jnp.zeros((64, E), BF16)
     for part in range(3):
         odd_v[pl.ds(256 * part + 240, 16), :] = jnp.zeros((16, E), BF16)
-    g_copy.wait()
     tell_below.wait()
     tell_above.wait()
 
@@ -332,6 +403,8 @@
     m0 = metric[pl.ds(0, 1), :]
     m1 = metric[pl.ds(1, 1), :]
     pace = step[...]
+
+    pending = []
 
     def send_halo(sweep):
         picked = dot(trace_halves[...], oh_halo[...])
@@ -375,6 +448,7 @@
             trace_halves[pl.ds(80 * k, 80), :] = high
             trace_halves[pl.ds(320 + 80 * k, 80), :] = low
         down, up = send_halo(sweep)
+        pending.extend((down, up))
 
         for k in range(4):
             got = dot(trace_halves[...], oh_local[:, E * k : E * (k + 1)])
@@ -387,8 +461,8 @@
         even_res[...] = dot(even_ops[pl.ds(240, 880), :], even_v[...])
         odd_res[...] = dot(odd_ops[pl.ds(240, 720), :], odd_v[...])
 
-        down.wait()
-        up.wait()
+        down.wait_recv()
+        up.wait_recv()
         ghost = jnp.concatenate([halo_in[sweep, 0], halo_in[sweep, 1]], axis=1)
         ghost_halves = jnp.concatenate(list(halves(ghost)), axis=0)
         for k in range(4):
@@ -438,41 +512,44 @@
 
     residual(0, next_field)
     residual(1, results)
-    copy_res = pltpu.make_async_copy(res_out, out_res, local_sem.at[3])
-    copy_two = pltpu.make_async_copy(two_out, out_two, local_sem.at[4])
-    copy_res.start()
-    copy_two.start()
     arrived.wait_send()
-    copy_res.wait()
-    copy_two.wait()
+    for copy in pending:
+        copy.wait_send()
+
+
+def hand_out(two, res, out_two, out_res, sem):
+    copies = [
+        pltpu.make_async_copy(two, out_two, sem.at[0]),
+        pltpu.make_async_copy(res, out_res, sem.at[1]),
+    ]
+    for copy in copies:
+        copy.start()
+    for copy in copies:
+        copy.wait()
 
 
 def shards(n, *args):
     (lam, order, send_index, recv_slot, grad, metric, step, coup, neighbour, neighbour_face, orient, halo_send) = args
-    in_vmem = pl.BlockSpec(memory_space=pltpu.VMEM)
     anywhere = pl.BlockSpec(memory_space=pl.ANY)
     shape = jax.ShapeDtypeStruct((F, M, M, E), F32)
-    return pl.pallas_call(
+    two, res = pl.pallas_call(
         functools.partial(kernel, n),
-        out_shape=(shape, shape),
-        in_specs=[
-            anywhere,
-            in_vmem,
-            in_vmem,
-            in_vmem,
-            anywhere,
-            in_vmem,
-            in_vmem,
-            in_vmem,
-            in_vmem,
-            in_vmem,
-            in_vmem,
-            in_vmem,
-        ],
-        out_specs=(anywhere, anywhere),
+        out_shape=(pltpu.VMEM((F, M, M, E), F32),) * 2,
+        in_specs=[pl.BlockSpec(memory_space=pltpu.HBM)] * 12,
+        out_specs=(pl.BlockSpec(memory_space=pltpu.VMEM),) * 2,
         scratch_shapes=[
             pltpu.VMEM((F, M, M, E), F32),
             pltpu.VMEM((F, M, M, E), F32),
+            pltpu.VMEM((1, E), jnp.int32),
+            pltpu.VMEM((1, E), jnp.int32),
+            pltpu.VMEM((1, E), jnp.int32),
+            pltpu.VMEM((2, E), F32),
+            pltpu.VMEM((1, E), F32),
+            pltpu.VMEM((F, 4, F), F32),
+            pltpu.VMEM((4, E), jnp.int32),
+            pltpu.VMEM((4, E), jnp.int32),
+            pltpu.VMEM((4, E), jnp.int32),
+            pltpu.VMEM((2, HALO), jnp.int32),
             pltpu.VMEM((E, E), F32),
             pltpu.VMEM((4 * E, 128), F32),
             pltpu.VMEM((4 * E, 128), F32),
@@ -495,9 +572,8 @@
             pltpu.VMEM((11 * BLOCK, E), F32),
             pltpu.VMEM((9 * BLOCK, E), F32),
             pltpu.VMEM((4, BLOCK, E), F32),
-            pltpu.VMEM((F, M, M, E), F32),
-            pltpu.VMEM((F, M, M, E), F32),
-            pltpu.SemaphoreType.DMA((5,)),
+            pltpu.SemaphoreType.DMA((12,)),
+            pltpu.SemaphoreType.DMA((1,)),
             pltpu.SemaphoreType.DMA,
             pltpu.SemaphoreType.DMA,
             pltpu.SemaphoreType.DMA((2,)),
@@ -506,7 +582,7 @@
             pltpu.SemaphoreType.DMA((2, 2)),
         ],
         compiler_params=pltpu.CompilerParams(
-            collective_id=0, has_side_effects=True, vmem_limit_bytes=48 * 1024 * 1024
+            collective_id=0, has_side_effects=True, vmem_limit_bytes=60928 * 1024
         ),
     )(
         lam,
@@ -516,12 +592,20 @@
         grad,
         metric,
         step.reshape(1, E),
-        coup,
+        jnp.transpose(coup, (1, 0, 2)),
         neighbour,
         neighbour_face,
         orient,
         halo_send,
     )
+    return pl.pallas_call(
+        hand_out,
+        out_shape=(shape, shape),
+        in_specs=[anywhere] * 2,
+        out_specs=(anywhere, anywhere),
+        scratch_shapes=[pltpu.SemaphoreType.DMA((2,))],
+        compiler_params=pltpu.CompilerParams(vmem_limit_bytes=1024 * 1024),
+    )(two, res)
 
 
 def solution(mesh):

time: 56.8 us -> 43.7 us (0.77)
  local copies, waits for them, and re-layouts: 11.4 us -> 0 us
  Pallas kernels: 44.2 us -> 43 us
    unnamed x25 -> x0, local copies, waits for them, and re-layouts: 11.4 us -> none
    pallas_call x1 -> x2, Pallas kernels: 44.2 us -> 43 us  [the longest x1 41.6 us: shards(): pl.pallas_call(functools.partial(kernel, n), out_shape=(pltpu.VMEM((F, M,...]
where the time goes in v1:
time: 43.7 us; the launch traced here: 43.6 us
  Pallas kernels  43 us (98%)
  between operations  0.64 us (1%)
    pallas_call x1, Pallas kernels, shards(): pl.pallas_call(functools.partial(kernel, n), out_shape=(pltpu.VMEM((F, M,...  41.6 us
    pallas_call x1, Pallas kernels, shards(): pl.pallas_call(hand_out, out_shape=(shape, shape), in_specs=[anywhere] *...  1.4 us

profile of v1, /device:TPU:0, one launch (start us, length us, event | category | flops | bytes accessed | tf_op | source)
XLA Modules:
  0.0 43.6 jit_solution(4851842104818902068)
XLA Ops:
  0.6 41.6 %shard_map.131 = (f32[10,7,7,512]{3,2,1,0:T(8,128)S(1)}, f32[10,7,7,512]{3,2,1,0:T(8,128)S(1)}) custom-call(f32[10,7,7,512]{3,2,1,0:T(8,128)} %lam.1, s32[1,512]{1,0:T(1,128)} %bitcast.4, s32[1,512]{1,0:T(1,128)} %send_far.1, s32[1,512]{1,0:T(1,128)} %recv_far.1, f32[10,7,7,512]{3,2,1,0:T(8,128)} %grad.1, f32[2,512]{1,0:T(2,128)} %metric_far.1, ...), custom_call_target="tpu_custom_call" | custom-call | tf_op jit(solution)/shard_map/pallas_call | solution.py:535
  42.2 1.4 %shard_map.132 = (f32[10,7,7,512]{3,2,1,0:T(8,128)}, f32[10,7,7,512]{3,2,1,0:T(8,128)}) custom-call(f32[10,7,7,512]{3,2,1,0:T(8,128)S(1)} %get-tuple-element.4.two, f32[10,7,7,512]{3,2,1,0:T(8,128)S(1)} %get-tuple-element.5.res), custom_call_target="tpu_custom_call" | custom-call | tf_op jit(solution)/shard_map/pallas_call | solution.py:601

commit v2 on v1

--- a/solution.py
+++ b/solution.py
@@ -163,6 +163,18 @@
     build(odd_ops, ODD, EVEN, store_odd)
 
 
+def residual_block(at, i, base, across, masks):
+    odd_row = (iota((8, E), 0) & 1) == 1
+    mask = masks[i]
+    parts = []
+    for f in range(F):
+        plus = jnp.broadcast_to(across[0, pl.ds(8 * f + i, 1), :], (8, E))
+        minus = jnp.broadcast_to(across[2, pl.ds(8 * f + i, 1), :], (8, E))
+        lift = jnp.where(odd_row, minus, plus) + across[1 if i % 2 == 0 else 3, pl.ds(8 * f, 8), :]
+        parts.append((base[pl.ds(BLOCK * at + 8 * f, 8), :] - lift) * mask)
+    return jnp.concatenate(parts, axis=0)
+
+
 def kernel(
     n,
     lam,
@@ -177,8 +189,11 @@
     face_far,
     orient_far,
     halo_far,
-    two_out,
-    res_out,
+    field,
+    base,
+    across,
+    masks,
+    pace_out,
     x_in,
     g_in,
     order,
@@ -198,12 +213,12 @@
     oh_local,
     oh_ghost,
     oh_halo,
+    oh_halo_arrived,
+    oh_local_arrived,
     even_ops,
     odd_ops,
     even_v,
     odd_v,
-    field,
-    masks,
     traces,
     trace_halves,
     faces_send,
@@ -212,7 +227,6 @@
     halo_in,
     even_res,
     odd_res,
-    across,
     input_sem,
     local_sem,
     move_send,
@@ -251,11 +265,23 @@
     for fetch in fetches:
         fetch.start()
 
-    def greet(j, carry):
-        pl.semaphore_signal(barrier, inc=1, device_id=(lax.rem(me + j, n),), device_id_type=pl.DeviceIdType.MESH)
-        return carry
-
-    lax.fori_loop(1, n, greet, 0)
+    sizes = (n // 32, 4, 4, 2) if n >= 32 else (1, 1, n // 2, 2)
+    core = lax.rem(me, 2)
+    partners = []
+    for offset in send_order(sizes):
+        p = lax.rem(core + offset[3], 2)
+        weight = 2
+        place = me // 2
+        for shift, size in zip(offset[2::-1], sizes[2::-1]):
+            here = lax.rem(place, size)
+            if shift:
+                here = lax.rem(here + jnp.where(core == 0, shift, size - shift), size)
+            p = p + weight * here
+            weight = weight * size
+            place = place // size
+        partners.append(p)
+    for p in partners:
+        pl.semaphore_signal(barrier, inc=1, device_id=(p,), device_id_type=pl.DeviceIdType.MESH)
 
     fetches[0].wait()
     fetches[1].wait()
@@ -271,47 +297,11 @@
     for part in range(4):
         send_buf[pl.ds(part, E, stride=4), :] = sorted_rows[:, 128 * part : 128 * (part + 1)]
 
-    pl.semaphore_wait(barrier, n - 1)
-
-    def piece(p):
-        return pl.ds(pl.multiple_of(p * chunk, chunk), chunk)
-
-    sizes = (n // 32, 4, 4, 2) if n >= 32 else (1, 1, n // 2, 2)
-    core = lax.rem(me, 2)
-    for offset in send_order(sizes):
-        p = lax.rem(core + offset[3], 2)
-        weight = 2
-        place = me // 2
-        for shift, size in zip(offset[2::-1], sizes[2::-1]):
-            here = lax.rem(place, size)
-            if shift:
-                here = lax.rem(here + jnp.where(core == 0, shift, size - shift), size)
-            p = p + weight * here
-            weight = weight * size
-            place = place // size
-        pltpu.make_async_remote_copy(
-            src_ref=send_buf.at[piece(p), :],
-            dst_ref=recv_buf.at[piece(me), :],
-            send_sem=move_send,
-            recv_sem=move_recv,
-            device_id=(p,),
-            device_id_type=pl.DeviceIdType.MESH,
-        ).start()
-    own = pltpu.make_async_copy(send_buf.at[piece(me), :], recv_buf.at[piece(me), :], local_sem.at[0])
-    own.start()
-
-    for fetch in fetches[3:]:
+    for fetch in fetches[3:5]:
         fetch.wait()
     rows = iota((E, E), 0)
     for k in range(4):
-        name = neighbour[pl.ds(k, 1), :]
-        oh_local[:, E * k : E * (k + 1)] = one_hot(rows == name)
-        oh_ghost[:, E * k : E * (k + 1)] = one_hot(rows == name - E)
-    for side in range(2):
-        oh_halo[:, HALO * side : HALO * (side + 1)] = one_hot(
-            iota((E, HALO), 0) == halo_send[pl.ds(side, 1), :]
-        )
-
+        oh_ghost[:, E * k : E * (k + 1)] = one_hot(rows == neighbour[pl.ds(k, 1), :] - E)
     wanted = jnp.zeros((16, E), F32)
     for k in range(4):
         face_row = jnp.broadcast_to(neighbour_face[pl.ds(k, 1), :].astype(F32), (16, E)).astype(BF16)
@@ -334,12 +324,46 @@
         device_id=(above,),
         device_id_type=pl.DeviceIdType.MESH,
     )
+    pl.semaphore_wait(barrier, n - 1)
     tell_below.start()
     tell_above.start()
 
+    def piece(p):
+        return pl.ds(pl.multiple_of(p * chunk, chunk), chunk)
+
+    def send(p):
+        pltpu.make_async_remote_copy(
+            src_ref=send_buf.at[piece(p), :],
+            dst_ref=recv_buf.at[piece(me), :],
+            send_sem=move_send,
+            recv_sem=move_recv,
+            device_id=(p,),
+            device_id_type=pl.DeviceIdType.MESH,
+        ).start()
+
+    for p in partners:
+        send(p)
+    own = pltpu.make_async_copy(send_buf.at[piece(me), :], recv_buf.at[piece(me), :], local_sem.at[0])
+    own.start()
+
+    for fetch in fetches[5:]:
+        fetch.wait()
+    for k in range(4):
+        name = neighbour[pl.ds(k, 1), :]
+        oh_local[:, E * k : E * (k + 1)] = one_hot(rows == name)
+    for side in range(2):
+        oh_halo[:, HALO * side : HALO * (side + 1)] = one_hot(
+            iota((E, HALO), 0) == halo_send[pl.ds(side, 1), :]
+        )
+
     oh_slot[...] = one_hot(column(recv_slot[...]) == iota((E, E), 1))
+    oh_halo_arrived[...] = dot(oh_slot[...], oh_halo[...]).astype(BF16)
+    for k in range(4):
+        lanes = slice(E * k, E * (k + 1))
+        oh_local_arrived[:, lanes] = dot(oh_slot[...], oh_local[:, lanes]).astype(BF16)
     build_operators(coup, even_ops, odd_ops)
     even_v[pl.ds(960, 64), :] = jnp.zeros((64, E), BF16)
+    base[...] = jnp.zeros((ROWS, E), F32)
     for part in range(3):
         odd_v[pl.ds(256 * part + 240, 16), :] = jnp.zeros((16, E), BF16)
     tell_below.wait()
@@ -357,15 +381,15 @@
     )
     arrived.wait_recv()
     for part in range(4):
-        flat = jnp.transpose(recv_buf[pl.ds(part, E, stride=4), :])
-        high, low = halves(flat)
-        compact[pl.ds(128 * part, 128), :] = dot(high, oh_slot[...]) + dot(low, oh_slot[...])
-
-    order_row = compact[pl.ds(F * M * M, 1), :]
-    lane_mode = iota((8, E), 0).astype(F32)
-    mask_j = jnp.where(lane_mode <= order_row, 1.0, 0.0)
-    for i in range(M):
-        masks[i] = jnp.where(order_row >= float(i), mask_j, 0.0)
+        compact[pl.ds(128 * part, 128), :] = jnp.transpose(recv_buf[pl.ds(part, E, stride=4), :])
+
+    mode_j = iota((8, E), 0).astype(F32)
+
+    def mode_masks(order_row):
+        mask_j = jnp.where(mode_j <= order_row, 1.0, 0.0)
+        return [jnp.where(order_row >= float(i), mask_j, 0.0) for i in range(M)]
+
+    order_arrived = compact[pl.ds(F * M * M, 1), :]
 
     def keep_halves(at, value):
         high, low = halves(value)
@@ -387,17 +411,40 @@
         odd_v[pl.ds(256 + BLOCK * at, BLOCK), :] = high
         odd_v[pl.ds(512 + BLOCK * at, BLOCK), :] = low
 
-    def set_field(at, value):
-        field[pl.ds(BLOCK * at, BLOCK), :] = value
+    def place_block(at, value):
         if at < 4:
             keep_halves(at, value)
         else:
             keep_odd_halves(at - 4, value)
 
+    masks_arrived = mode_masks(order_arrived)
     for at, i in enumerate(PLACE):
-        mask = masks[i]
-        parts = [compact[pl.ds(M * (at * F + f), 8), :] * mask for f in range(F)]
-        set_field(at, jnp.concatenate(parts, axis=0))
+        parts = [compact[pl.ds(M * (at * F + f), 8), :] * masks_arrived[i] for f in range(F)]
+        place_block(at, jnp.concatenate(parts, axis=0))
+
+    def set_field(at, value):
+        field[pl.ds(BLOCK * at, BLOCK), :] = value
+        place_block(at, value)
+
+    def take_slots():
+        order_rows = jnp.broadcast_to(order_arrived, (16, E)).astype(BF16)
+        order_row = dot(order_rows, oh_slot[...])[0:1]
+        for i, mask in enumerate(mode_masks(order_row)):
+            masks[i] = mask
+        high = jnp.concatenate([even_v[pl.ds(0, 320), :], odd_v[pl.ds(0, 240), :]], axis=0)
+        low = jnp.concatenate([even_v[pl.ds(640, 320), :], odd_v[pl.ds(512, 240), :]], axis=0)
+        high = dot(high, oh_slot[...])
+        low = dot(low, oh_slot[...])
+        field[...] = high + low
+        high = high.astype(BF16)
+        low = low.astype(BF16)
+        even_v[pl.ds(0, 320), :] = high[0:320]
+        even_v[pl.ds(320, 64), :] = high[256:320]
+        even_v[pl.ds(384, 256), :] = high[0:256]
+        even_v[pl.ds(640, 320), :] = low[0:320]
+        odd_v[pl.ds(0, 240), :] = high[320:560]
+        odd_v[pl.ds(256, 240), :] = high[320:560]
+        odd_v[pl.ds(512, 240), :] = low[320:560]
 
     odd_row = (iota((8, E), 0) & 1) == 1
     m0 = metric[pl.ds(0, 1), :]
@@ -406,8 +453,8 @@
 
     pending = []
 
-    def send_halo(sweep):
-        picked = dot(trace_halves[...], oh_halo[...])
+    def send_halo(sweep, chosen_halo):
+        picked = dot(trace_halves[...], chosen_halo[...])
         picked = picked[0:320] + picked[320:640]
         for side in range(2):
             face = faces_recv[side][0:1, :]
@@ -436,7 +483,21 @@
         up.start()
         return down, up
 
-    def residual(sweep, finish):
+    def turned(k):
+        sign = jnp.where(odd_row & (orient[pl.ds(k, 1), :] == 1), -1.0, 1.0)
+        return jnp.concatenate([sign] * F, axis=0)
+
+    def combine(across):
+        south = across[0]
+        north = across[2]
+        across[0] = north + south
+        across[2] = north - south
+        east = across[1]
+        west = across[3]
+        across[1] = east + west
+        across[3] = east - west
+
+    def residual(sweep, chosen_halo, chosen_local, before_volume, finish):
         from_even = dot(even_ops[pl.ds(0, 240), :], even_v[...])
         from_odd = dot(odd_ops[pl.ds(0, 240), :], odd_v[...])
         traces[0] = from_even[80:160] + from_odd[80:160]
@@ -447,37 +508,21 @@
             high, low = halves(traces[k])
             trace_halves[pl.ds(80 * k, 80), :] = high
             trace_halves[pl.ds(320 + 80 * k, 80), :] = low
-        down, up = send_halo(sweep)
+        down, up = send_halo(sweep, chosen_halo)
         pending.extend((down, up))
 
         for k in range(4):
-            got = dot(trace_halves[...], oh_local[:, E * k : E * (k + 1)])
+            got = dot(trace_halves[...], chosen_local[:, E * k : E * (k + 1)])
             got = got[0:320] + got[320:640]
             face = neighbour_face[pl.ds(k, 1), :]
             chosen = got[240:320]
             for other in (2, 1, 0):
                 chosen = jnp.where(face == other, got[80 * other : 80 * (other + 1)], chosen)
-            across[k] = chosen
+            across[k] = chosen * turned(k)
+        combine(across)
+        before_volume()
         even_res[...] = dot(even_ops[pl.ds(240, 880), :], even_v[...])
         odd_res[...] = dot(odd_ops[pl.ds(240, 720), :], odd_v[...])
-
-        down.wait_recv()
-        up.wait_recv()
-        ghost = jnp.concatenate([halo_in[sweep, 0], halo_in[sweep, 1]], axis=1)
-        ghost_halves = jnp.concatenate(list(halves(ghost)), axis=0)
-        for k in range(4):
-            got = dot(ghost_halves, oh_ghost[:, E * k : E * (k + 1)])
-            turned = jnp.where(odd_row & (orient[pl.ds(k, 1), :] == 1), -1.0, 1.0)
-            turned = jnp.concatenate([turned] * F, axis=0)
-            across[k] = (across[k] + got[0:80] + got[80:160]) * turned
-        south = across[0]
-        north = across[2]
-        across[0] = north + south
-        across[2] = north - south
-        east = across[1]
-        west = across[3]
-        across[1] = east + west
-        across[3] = east - west
 
         for at, i in enumerate(PLACE):
             if i % 2 == 0:
@@ -485,45 +530,52 @@
                 here = here + even_res[pl.ds(560 + BLOCK * at, BLOCK), :]
                 if i > 0:
                     here = here + m0 * odd_res[pl.ds(BLOCK * (at - 1), BLOCK), :]
-                here = here - across[1]
             else:
                 here = m1 * odd_res[pl.ds(240 + BLOCK * (at - 4), BLOCK), :]
                 here = here + odd_res[pl.ds(480 + BLOCK * (at - 4), BLOCK), :]
                 here = here + m0 * even_res[pl.ds(BLOCK * (at - 4), BLOCK), :]
-                here = here - across[3]
-            mask = masks[i]
-            parts = []
             for f in range(F):
-                plus = jnp.broadcast_to(across[0, pl.ds(8 * f + i, 1), :], (8, E))
-                minus = jnp.broadcast_to(across[2, pl.ds(8 * f + i, 1), :], (8, E))
-                lift = jnp.where(odd_row, minus, plus)
-                goal = jnp.concatenate([g_in[f, i], jnp.zeros((1, E), F32)], axis=0)
-                parts.append((here[8 * f : 8 * f + 8] - lift - goal) * mask)
-            value = jnp.concatenate(parts, axis=0)
-            finish(at, i, value, field[pl.ds(BLOCK * at, BLOCK), :] - pace * value)
-
-    def next_field(at, i, value, advanced):
-        set_field(at, advanced)
-
-    def results(at, i, value, advanced):
-        for f in range(F):
-            res_out[f, i] = value[8 * f : 8 * f + M]
-            two_out[f, i] = advanced[8 * f : 8 * f + M]
-
-    residual(0, next_field)
-    residual(1, results)
+                base[pl.ds(BLOCK * at + 8 * f, M), :] = here[8 * f : 8 * f + M] - g_in[f, i]
+
+        down.wait_recv()
+        up.wait_recv()
+        ghost = jnp.concatenate([halo_in[sweep, 0], halo_in[sweep, 1]], axis=1)
+        ghost_halves = jnp.concatenate(list(halves(ghost)), axis=0)
+        beyond = []
+        for k in range(4):
+            got = dot(ghost_halves, oh_ghost[:, E * k : E * (k + 1)])
+            beyond.append((got[0:80] + got[80:160]) * turned(k))
+        across[0] = across[0] + (beyond[2] + beyond[0])
+        across[2] = across[2] + (beyond[2] - beyond[0])
+        across[1] = across[1] + (beyond[1] + beyond[3])
+        across[3] = across[3] + (beyond[1] - beyond[3])
+
+        finish()
+
+    def next_field():
+        for at, i in enumerate(PLACE):
+            value = residual_block(at, i, base, across, masks)
+            set_field(at, field[pl.ds(BLOCK * at, BLOCK), :] - pace * value)
+
+    residual(0, oh_halo_arrived, oh_local_arrived, take_slots, next_field)
+    residual(1, oh_halo, oh_local, lambda: None, lambda: None)
+    pace_out[...] = pace
     arrived.wait_send()
     for copy in pending:
         copy.wait_send()
 
 
-def hand_out(two, res, out_two, out_res, sem):
-    copies = [
-        pltpu.make_async_copy(two, out_two, sem.at[0]),
-        pltpu.make_async_copy(res, out_res, sem.at[1]),
-    ]
-    for copy in copies:
-        copy.start()
+def last_step(field, base, across, masks, pace, out_two, out_res, two, res, sem):
+    copies = []
+    for at, i in enumerate(PLACE):
+        value = residual_block(at, i, base, across, masks)
+        advanced = field[pl.ds(BLOCK * at, BLOCK), :] - pace[...] * value
+        for f in range(F):
+            res[f, i] = value[8 * f : 8 * f + M]
+            two[f, i] = advanced[8 * f : 8 * f + M]
+        for kind, (near, far) in enumerate(((two, out_two), (res, out_res))):
+            copies.append(pltpu.make_async_copy(near.at[:, i], far.at[:, i], sem.at[kind, i]))
+            copies[-1].start()
     for copy in copies:
         copy.wait()
 
@@ -532,11 +584,17 @@
     (lam, order, send_index, recv_slot, grad, metric, step, coup, neighbour, neighbour_face, orient, halo_send) = args
     anywhere = pl.BlockSpec(memory_space=pl.ANY)
     shape = jax.ShapeDtypeStruct((F, M, M, E), F32)
-    two, res = pl.pallas_call(
+    kept = pl.pallas_call(
         functools.partial(kernel, n),
-        out_shape=(pltpu.VMEM((F, M, M, E), F32),) * 2,
+        out_shape=(
+            pltpu.VMEM((ROWS, E), F32),
+            pltpu.VMEM((ROWS, E), F32),
+            pltpu.VMEM((4, BLOCK, E), F32),
+            pltpu.VMEM((M, 8, E), F32),
+            pltpu.VMEM((1, E), F32),
+        ),
         in_specs=[pl.BlockSpec(memory_space=pltpu.HBM)] * 12,
-        out_specs=(pl.BlockSpec(memory_space=pltpu.VMEM),) * 2,
+        out_specs=(pl.BlockSpec(memory_space=pltpu.VMEM),) * 5,
         scratch_shapes=[
             pltpu.VMEM((F, M, M, E), F32),
             pltpu.VMEM((F, M, M, E), F32),
@@ -557,12 +615,12 @@
             pltpu.VMEM((E, 4 * E), BF16),
             pltpu.VMEM((E, 4 * E), BF16),
             pltpu.VMEM((E, E), BF16),
+            pltpu.VMEM((E, E), BF16),
+            pltpu.VMEM((E, 4 * E), BF16),
             pltpu.VMEM((14 * BLOCK, 1024), BF16),
             pltpu.VMEM((12 * BLOCK, 768), BF16),
             pltpu.VMEM((1024, E), BF16),
             pltpu.VMEM((768, E), BF16),
-            pltpu.VMEM((ROWS, E), F32),
-            pltpu.VMEM((M, 8, E), F32),
             pltpu.VMEM((4, BLOCK, E), F32),
             pltpu.VMEM((8 * BLOCK, E), BF16),
             pltpu.VMEM((2, 8, HALO), F32),
@@ -571,7 +629,6 @@
             pltpu.VMEM((2, 2, BLOCK, HALO), F32),
             pltpu.VMEM((11 * BLOCK, E), F32),
             pltpu.VMEM((9 * BLOCK, E), F32),
-            pltpu.VMEM((4, BLOCK, E), F32),
             pltpu.SemaphoreType.DMA((12,)),
             pltpu.SemaphoreType.DMA((1,)),
             pltpu.SemaphoreType.DMA,
@@ -599,13 +656,17 @@
         halo_send,
     )
     return pl.pallas_call(
-        hand_out,
+        last_step,
         out_shape=(shape, shape),
-        in_specs=[anywhere] * 2,
+        in_specs=[pl.BlockSpec(memory_space=pltpu.VMEM)] * 5,
         out_specs=(anywhere, anywhere),
-        scratch_shapes=[pltpu.SemaphoreType.DMA((2,))],
-        compiler_params=pltpu.CompilerParams(vmem_limit_bytes=1024 * 1024),
-    )(two, res)
+        scratch_shapes=[
+            pltpu.VMEM((F, M, M, E), F32),
+            pltpu.VMEM((F, M, M, E), F32),
+            pltpu.SemaphoreType.DMA((2, M)),
+        ],
+        compiler_params=pltpu.CompilerParams(vmem_limit_bytes=4 * 1024 * 1024),
+    )(*kept)
 
 
 def solution(mesh):

time: 43.7 us -> 41.5 us (0.950)
  Pallas kernels: 43 us -> 40.6 us
    pallas_call x2, Pallas kernels: 43 us -> 40.6 us  [the longest x1 39 us: shards(): pl.pallas_call(functools.partial(kernel, n), out_shape=(pltpu.VMEM((ROWS,...]
where the time goes in v2:
time: 41.5 us; the launch traced here: 41.4 us
  Pallas kernels  40.6 us (98%)
  between operations  0.8 us (2%)
    pallas_call x1, Pallas kernels, shards(): pl.pallas_call(functools.partial(kernel, n), out_shape=(pltpu.VMEM((ROWS,...  39 us
    pallas_call x1, Pallas kernels, shards(): pl.pallas_call(last_step, out_shape=(shape, shape), in_specs=[pl.BlockSpe...  1.54 us

profile of v2, /device:TPU:0, one launch (start us, length us, event | category | flops | bytes accessed | tf_op | source)
XLA Modules:
  0.0 41.4 jit_solution(3554676452738453054)
XLA Ops:
  0.6 39.0 %shard_map.131 = (f32[560,512]{1,0:T(8,128)S(1)}, f32[560,512]{1,0:T(8,128)S(1)}, f32[4,80,512]{2,1,0:T(8,128)S(1)}, f32[7,8,512]{2,1,0:T(8,128)S(1)}, f32[1,512]{1,0:T(1,128)S(1)}) custom-call(f32[10,7,7,512]{3,2,1,0:T(8,128)} %lam.1, s32[1,512]{1,0:T(1,128)} %bitcast.4, s32[1,512]{1,0:T(1,128)} %send_far.1, s32[1,512]{1,0:T(1,128)} %recv_far.1, ...), custom_call_target="tpu_custom_call" | custom-call | tf_op jit(solution)/shard_map/pallas_call | solution.py:587
  39.7 1.5 %shard_map.132 = (f32[10,7,7,512]{3,2,1,0:T(8,128)}, f32[10,7,7,512]{3,2,1,0:T(8,128)}) custom-call(f32[560,512]{1,0:T(8,128)S(1)} %get-tuple-element.7.field, f32[560,512]{1,0:T(8,128)S(1)} %get-tuple-element.8.base, f32[4,80,512]{2,1,0:T(8,128)S(1)} %get-tuple-element.9.across, f32[7,8,512]{2,1,0:T(8,128)S(1)} %get-tuple-element.10.masks, ...), custom_call_target="tpu_custom_call" | custom-call | tf_op jit(solution)/shard_map/pallas_call | solution.py:658

commit v3 on v2

--- a/solution.py
+++ b/solution.py
@@ -241,21 +241,24 @@
     chunk = 4 * cap
     above = lax.rem(me + 1, n)
     below = lax.rem(me + n - 1, n)
+    core = lax.rem(me, 2)
+    far = jnp.where(core == 0, below, above)
+    near = jnp.where(core == 0, above, below)
     barrier = pltpu.get_barrier_semaphore()
 
     fetches = [
-        pltpu.make_async_copy(far, near, input_sem.at[at])
-        for at, (far, near) in enumerate(
+        pltpu.make_async_copy(source, target, input_sem.at[at])
+        for at, (source, target) in enumerate(
             (
                 (send_far, send_index),
                 (order_far, order),
                 (lam, x_in),
                 (neighbour_far, neighbour),
                 (face_far, neighbour_face),
+                (orient_far, orient),
                 (halo_far, halo_send),
                 (recv_far, recv_slot),
                 (coup_far, coup),
-                (orient_far, orient),
                 (metric_far, metric),
                 (step_far, step),
                 (grad, g_in),
@@ -266,7 +269,6 @@
         fetch.start()
 
     sizes = (n // 32, 4, 4, 2) if n >= 32 else (1, 1, n // 2, 2)
-    core = lax.rem(me, 2)
     partners = []
     for offset in send_order(sizes):
         p = lax.rem(core + offset[3], 2)
@@ -297,36 +299,32 @@
     for part in range(4):
         send_buf[pl.ds(part, E, stride=4), :] = sorted_rows[:, 128 * part : 128 * (part + 1)]
 
-    for fetch in fetches[3:5]:
+    for fetch in fetches[3:6]:
         fetch.wait()
     rows = iota((E, E), 0)
     for k in range(4):
-        oh_ghost[:, E * k : E * (k + 1)] = one_hot(rows == neighbour[pl.ds(k, 1), :] - E)
+        oh_ghost[:, E * k : E * (k + 1)] = one_hot(rows == ((neighbour[pl.ds(k, 1), :] - E) ^ (HALO * core)))
     wanted = jnp.zeros((16, E), F32)
     for k in range(4):
-        face_row = jnp.broadcast_to(neighbour_face[pl.ds(k, 1), :].astype(F32), (16, E)).astype(BF16)
-        wanted = wanted + dot(face_row, oh_ghost[:, E * k : E * (k + 1)], NT)
+        code = neighbour_face[pl.ds(k, 1), :] + 4 * orient[pl.ds(k, 1), :]
+        code = jnp.broadcast_to(code.astype(F32), (16, E)).astype(BF16)
+        wanted = wanted + dot(code, oh_ghost[:, E * k : E * (k + 1)], NT)
     faces_send[0] = wanted[0:8, 0:HALO]
     faces_send[1] = wanted[0:8, HALO:E]
-    tell_below = pltpu.make_async_remote_copy(
-        src_ref=faces_send.at[0],
-        dst_ref=faces_recv.at[1],
-        send_sem=face_send_sem.at[0],
-        recv_sem=face_recv_sem.at[1],
-        device_id=(below,),
-        device_id_type=pl.DeviceIdType.MESH,
-    )
-    tell_above = pltpu.make_async_remote_copy(
-        src_ref=faces_send.at[1],
-        dst_ref=faces_recv.at[0],
-        send_sem=face_send_sem.at[1],
-        recv_sem=face_recv_sem.at[0],
-        device_id=(above,),
-        device_id_type=pl.DeviceIdType.MESH,
-    )
+    tells = [
+        pltpu.make_async_remote_copy(
+            src_ref=faces_send.at[side],
+            dst_ref=faces_recv.at[side],
+            send_sem=face_send_sem.at[side],
+            recv_sem=face_recv_sem.at[side],
+            device_id=(whom,),
+            device_id_type=pl.DeviceIdType.MESH,
+        )
+        for side, whom in enumerate((far, near))
+    ]
     pl.semaphore_wait(barrier, n - 1)
-    tell_below.start()
-    tell_above.start()
+    for tell in tells:
+        tell.start()
 
     def piece(p):
         return pl.ds(pl.multiple_of(p * chunk, chunk), chunk)
@@ -346,16 +344,19 @@
     own = pltpu.make_async_copy(send_buf.at[piece(me), :], recv_buf.at[piece(me), :], local_sem.at[0])
     own.start()
 
-    for fetch in fetches[5:]:
+    for fetch in fetches[6:]:
         fetch.wait()
     for k in range(4):
         name = neighbour[pl.ds(k, 1), :]
         oh_local[:, E * k : E * (k + 1)] = one_hot(rows == name)
     for side in range(2):
         oh_halo[:, HALO * side : HALO * (side + 1)] = one_hot(
-            iota((E, HALO), 0) == halo_send[pl.ds(side, 1), :]
+            iota((E, HALO), 0) == halo_send[pl.ds(core if side == 0 else 1 - core, 1), :]
         )
 
+    south, east, north, west = (oh_ghost[:, E * k : E * (k + 1)].astype(F32) for k in range(4))
+    for at, both in enumerate((north + south, east + west, north - south, east - west)):
+        oh_ghost[:, E * at : E * (at + 1)] = both.astype(BF16)
     oh_slot[...] = one_hot(column(recv_slot[...]) == iota((E, E), 1))
     oh_halo_arrived[...] = dot(oh_slot[...], oh_halo[...]).astype(BF16)
     for k in range(4):
@@ -366,8 +367,8 @@
     base[...] = jnp.zeros((ROWS, E), F32)
     for part in range(3):
         odd_v[pl.ds(256 * part + 240, 16), :] = jnp.zeros((16, E), BF16)
-    tell_below.wait()
-    tell_above.wait()
+    for tell in tells:
+        tell.wait()
 
     own.wait()
     everyone = pl.ds(0, (n - 1) * chunk)
@@ -454,34 +455,30 @@
     pending = []
 
     def send_halo(sweep, chosen_halo):
-        picked = dot(trace_halves[...], chosen_halo[...])
-        picked = picked[0:320] + picked[320:640]
-        for side in range(2):
-            face = faces_recv[side][0:1, :]
-            lanes = slice(HALO * side, HALO * (side + 1))
-            chosen = picked[240:320, lanes]
+        copies = []
+        for side, whom in enumerate((far, near)):
+            picked = dot(trace_halves[...], chosen_halo[:, HALO * side : HALO * (side + 1)])
+            picked = picked[0:320] + picked[320:640]
+            code = faces_recv[side][0:1, :]
+            flipped = code >= 4.0
+            face = jnp.where(flipped, code - 4.0, code)
+            chosen = picked[240:320]
             for k in (2, 1, 0):
-                chosen = jnp.where(face == float(k), picked[80 * k : 80 * (k + 1), lanes], chosen)
-            halo_out[sweep, side] = chosen
-        down = pltpu.make_async_remote_copy(
-            src_ref=halo_out.at[sweep, 0],
-            dst_ref=halo_in.at[sweep, 1],
-            send_sem=halo_send_sem.at[sweep, 0],
-            recv_sem=halo_recv_sem.at[sweep, 1],
-            device_id=(below,),
-            device_id_type=pl.DeviceIdType.MESH,
-        )
-        up = pltpu.make_async_remote_copy(
-            src_ref=halo_out.at[sweep, 1],
-            dst_ref=halo_in.at[sweep, 0],
-            send_sem=halo_send_sem.at[sweep, 1],
-            recv_sem=halo_recv_sem.at[sweep, 0],
-            device_id=(above,),
-            device_id_type=pl.DeviceIdType.MESH,
-        )
-        down.start()
-        up.start()
-        return down, up
+                chosen = jnp.where(face == float(k), picked[80 * k : 80 * (k + 1)], chosen)
+            sign = jnp.where(odd_row[:, 0:HALO] & flipped, -1.0, 1.0)
+            halo_out[sweep, side] = chosen * jnp.concatenate([sign] * F, axis=0)
+            copies.append(
+                pltpu.make_async_remote_copy(
+                    src_ref=halo_out.at[sweep, side],
+                    dst_ref=halo_in.at[sweep, side],
+                    send_sem=halo_send_sem.at[sweep, side],
+                    recv_sem=halo_recv_sem.at[sweep, side],
+                    device_id=(whom,),
+                    device_id_type=pl.DeviceIdType.MESH,
+                )
+            )
+            copies[-1].start()
+        return copies
 
     def turned(k):
         sign = jnp.where(odd_row & (orient[pl.ds(k, 1), :] == 1), -1.0, 1.0)
@@ -508,8 +505,8 @@
             high, low = halves(traces[k])
             trace_halves[pl.ds(80 * k, 80), :] = high
             trace_halves[pl.ds(320 + 80 * k, 80), :] = low
-        down, up = send_halo(sweep, chosen_halo)
-        pending.extend((down, up))
+        sent = send_halo(sweep, chosen_halo)
+        pending.extend(sent)
 
         for k in range(4):
             got = dot(trace_halves[...], chosen_local[:, E * k : E * (k + 1)])
@@ -537,18 +534,12 @@
             for f in range(F):
                 base[pl.ds(BLOCK * at + 8 * f, M), :] = here[8 * f : 8 * f + M] - g_in[f, i]
 
-        down.wait_recv()
-        up.wait_recv()
-        ghost = jnp.concatenate([halo_in[sweep, 0], halo_in[sweep, 1]], axis=1)
-        ghost_halves = jnp.concatenate(list(halves(ghost)), axis=0)
-        beyond = []
-        for k in range(4):
-            got = dot(ghost_halves, oh_ghost[:, E * k : E * (k + 1)])
-            beyond.append((got[0:80] + got[80:160]) * turned(k))
-        across[0] = across[0] + (beyond[2] + beyond[0])
-        across[2] = across[2] + (beyond[2] - beyond[0])
-        across[1] = across[1] + (beyond[1] + beyond[3])
-        across[3] = across[3] + (beyond[1] - beyond[3])
+        for side in (1, 0):
+            sent[side].wait_recv()
+            ghost_halves = jnp.concatenate(list(halves(halo_in[sweep, side])), axis=0)
+            for at in range(4):
+                got = dot(ghost_halves, oh_ghost[HALO * side : HALO * (side + 1), E * at : E * (at + 1)])
+                across[at] = across[at] + (got[0:80] + got[80:160])
 
         finish()
 

time: 41.5 us -> 40.6 us (0.978)
  Pallas kernels: 40.6 us -> 39.7 us
    pallas_call x1, Pallas kernels: 39 us -> 38.1 us  [shards(): pl.pallas_call(functools.partial(kernel, n), out_shape=(pltpu.VMEM((ROWS,...]
where the time goes in v3:
time: 40.6 us; the launch traced here: 40.5 us
  Pallas kernels  39.7 us (98%)
  between operations  0.8 us (2%)
    pallas_call x1, Pallas kernels, shards(): pl.pallas_call(functools.partial(kernel, n), out_shape=(pltpu.VMEM((ROWS,...  38.1 us
    pallas_call x1, Pallas kernels, shards(): pl.pallas_call(last_step, out_shape=(shape, shape), in_specs=[pl.BlockSpe...  1.54 us

profile of v3, /device:TPU:0, one launch (start us, length us, event | category | flops | bytes accessed | tf_op | source)
XLA Modules:
  0.0 40.5 jit_solution(12399761226473449712)
XLA Ops:
  0.6 38.1 %shard_map.131 = (f32[560,512]{1,0:T(8,128)S(1)}, f32[560,512]{1,0:T(8,128)S(1)}, f32[4,80,512]{2,1,0:T(8,128)S(1)}, f32[7,8,512]{2,1,0:T(8,128)S(1)}, f32[1,512]{1,0:T(1,128)S(1)}) custom-call(f32[10,7,7,512]{3,2,1,0:T(8,128)} %lam.1, s32[1,512]{1,0:T(1,128)} %bitcast.4, s32[1,512]{1,0:T(1,128)} %send_far.1, s32[1,512]{1,0:T(1,128)} %recv_far.1, ...), custom_call_target="tpu_custom_call" | custom-call | tf_op jit(solution)/shard_map/pallas_call | solution.py:578
  38.8 1.5 %shard_map.132 = (f32[10,7,7,512]{3,2,1,0:T(8,128)}, f32[10,7,7,512]{3,2,1,0:T(8,128)}) custom-call(f32[560,512]{1,0:T(8,128)S(1)} %get-tuple-element.7.field, f32[560,512]{1,0:T(8,128)S(1)} %get-tuple-element.8.base, f32[4,80,512]{2,1,0:T(8,128)S(1)} %get-tuple-element.9.across, f32[7,8,512]{2,1,0:T(8,128)S(1)} %get-tuple-element.10.masks, ...), custom_call_target="tpu_custom_call" | custom-call | tf_op jit(solution)/shard_map/pallas_call | solution.py:649

commit v4 on v3

--- a/solution.py
+++ b/solution.py
@@ -423,9 +423,12 @@
         parts = [compact[pl.ds(M * (at * F + f), 8), :] * masks_arrived[i] for f in range(F)]
         place_block(at, jnp.concatenate(parts, axis=0))
 
-    def set_field(at, value):
-        field[pl.ds(BLOCK * at, BLOCK), :] = value
-        place_block(at, value)
+    def keep_field():
+        for at in range(M):
+            rows = pl.ds(BLOCK * at if at < 4 else BLOCK * (at - 4), BLOCK)
+            low_rows = pl.ds(640 + BLOCK * at if at < 4 else 512 + BLOCK * (at - 4), BLOCK)
+            source = even_v if at < 4 else odd_v
+            field[pl.ds(BLOCK * at, BLOCK), :] = source[rows, :].astype(F32) + source[low_rows, :].astype(F32)
 
     def take_slots():
         order_rows = jnp.broadcast_to(order_arrived, (16, E)).astype(BF16)
@@ -546,10 +549,10 @@
     def next_field():
         for at, i in enumerate(PLACE):
             value = residual_block(at, i, base, across, masks)
-            set_field(at, field[pl.ds(BLOCK * at, BLOCK), :] - pace * value)
+            place_block(at, field[pl.ds(BLOCK * at, BLOCK), :] - pace * value)
 
     residual(0, oh_halo_arrived, oh_local_arrived, take_slots, next_field)
-    residual(1, oh_halo, oh_local, lambda: None, lambda: None)
+    residual(1, oh_halo, oh_local, keep_field, lambda: None)
     pace_out[...] = pace
     arrived.wait_send()
     for copy in pending:

time: 40.6 us -> 40.6 us (level)
  no operation moved by 1% of the time
where the time goes in v4:
time: 40.6 us; the launch traced here: 40.5 us
  Pallas kernels  39.7 us (98%)
  between operations  0.8 us (2%)
    pallas_call x1, Pallas kernels, shards(): pl.pallas_call(functools.partial(kernel, n), out_shape=(pltpu.VMEM((ROWS,...  38.2 us
    pallas_call x1, Pallas kernels, shards(): pl.pallas_call(last_step, out_shape=(shape, shape), in_specs=[pl.BlockSpe...  1.54 us

profile of v4, /device:TPU:0, one launch (start us, length us, event | category | flops | bytes accessed | tf_op | source)
XLA Modules:
  0.0 40.5 jit_solution(14681992313031327755)
XLA Ops:
  0.6 38.2 %shard_map.131 = (f32[560,512]{1,0:T(8,128)S(1)}, f32[560,512]{1,0:T(8,128)S(1)}, f32[4,80,512]{2,1,0:T(8,128)S(1)}, f32[7,8,512]{2,1,0:T(8,128)S(1)}, f32[1,512]{1,0:T(1,128)S(1)}) custom-call(f32[10,7,7,512]{3,2,1,0:T(8,128)} %lam.1, s32[1,512]{1,0:T(1,128)} %bitcast.4, s32[1,512]{1,0:T(1,128)} %send_far.1, s32[1,512]{1,0:T(1,128)} %recv_far.1, ...), custom_call_target="tpu_custom_call" | custom-call | tf_op jit(solution)/shard_map/pallas_call | solution.py:581
  38.8 1.5 %shard_map.132 = (f32[10,7,7,512]{3,2,1,0:T(8,128)}, f32[10,7,7,512]{3,2,1,0:T(8,128)}) custom-call(f32[560,512]{1,0:T(8,128)S(1)} %get-tuple-element.7.field, f32[560,512]{1,0:T(8,128)S(1)} %get-tuple-element.8.base, f32[4,80,512]{2,1,0:T(8,128)S(1)} %get-tuple-element.9.across, f32[7,8,512]{2,1,0:T(8,128)S(1)} %get-tuple-element.10.masks, ...), custom_call_target="tpu_custom_call" | custom-call | tf_op jit(solution)/shard_map/pallas_call | solution.py:652
